TPU v7x, 32 devices: a whole 2x2x4 slice. The times are simulated.
32 devices in a mesh: tier: 4 (over x, core), tile: 8 (over z, y).
Axes of the slice: x: 2, y: 2, z: 4, core: 2. Of those that a mesh axis runs over, the one named last changes fastest.
Arguments:
- starting_warmth_rise: float32 [32, 96, 1024], P('tile', 'tier'), may hold values from -3 to 8
- substance_per_cell: int32 [32, 96, 1024], P('tile', 'tier'), may hold values from 0 to 7
- material_transport_rates: float32 [2, 8], replicated, may hold values from 0.2 to 2
- patch_region_label: int32 [8, 8], P('tile'), may hold values from 0 to 15, as said below
- static_power_per_area: float32 [4, 16], replicated, may hold values from 0.5 to 4
- warming_power_factor: float32 [4, 16], replicated, may hold values from 0.2 to 0.8
- stacking_solve_operator: float32 [96, 96], replicated, may hold values from 0 to 1
Outputs:
- final_temperature: float32 [32, 96, 1024], P('tile', 'tier')
- block_power: float32 [4, 16], P('tier')
Inputs may be any that keep to these rules, and one draw needn't show every extreme that they name: `patch_region_label`: every block number names at least one tile.
All inputs are finite; a program needn't handle non-finite values.
Results may differ from a plain program's by a relative error of at most 0.0001.
Values sent between devices are 32-bit elements; how exact they have to be, the bound alone decides.
A program may use at most 64 MiB of HBM per device.

v0:
```python
import jax
import jax.numpy as jnp
from jax import lax
from jax.sharding import PartitionSpec as P

TILE_COLS = 128
STEPS = 2
LATERAL_RATE = 0.12
SOURCE_GAIN = 0.02


def extended(block, sides, width):
    for axis, dim in sides:
        count = lax.axis_size(axis)
        forward = [(i, i + 1) for i in range(count - 1)]
        backward = [(target, source) for source, target in forward]
        low = lax.ppermute(
            lax.slice_in_dim(block, block.shape[dim] - width, None, axis=dim), axis, forward
        )
        high = lax.ppermute(lax.slice_in_dim(block, 0, width, axis=dim), axis, backward)
        block = jnp.concatenate([low, block, high], axis=dim)
    return block


def pair_mean(cond_a, cond_b):
    return 2.0 * cond_a * cond_b / (cond_a + cond_b)


def lateral(padded, conduct):
    centre = padded[1:-1, :, 1:-1]
    sideways_coupling_rate = conduct[0, 1:-1, :, 1:-1]
    stacking_coupling_rate = conduct[1, 1:-1, :, 1:-1]
    flow_sum = pair_mean(sideways_coupling_rate, conduct[0, 2:, :, 1:-1]) * (
        padded[2:, :, 1:-1] - centre
    )
    flow_sum = flow_sum + pair_mean(sideways_coupling_rate, conduct[0, :-2, :, 1:-1]) * (
        padded[:-2, :, 1:-1] - centre
    )
    flow_sum = flow_sum + pair_mean(stacking_coupling_rate, conduct[1, 1:-1, :, 2:]) * (
        padded[1:-1, :, 2:] - centre
    )
    flow_sum = flow_sum + pair_mean(stacking_coupling_rate, conduct[1, 1:-1, :, :-2]) * (
        padded[1:-1, :, :-2] - centre
    )
    return centre + LATERAL_RATE * flow_sum


def exact_dot(left_op, right_op):
    return jnp.dot(
        left_op, right_op, precision=lax.Precision.HIGHEST, preferred_element_type=jnp.float32
    )


def lookup_codes(codes, material_transport_rates):
    sideways_coupling_rate = jnp.zeros(codes.shape, jnp.float32)
    stacking_coupling_rate = jnp.zeros(codes.shape, jnp.float32)
    for material in range(material_transport_rates.shape[1]):
        is_material = codes == material + 1
        sideways_coupling_rate = jnp.where(
            is_material, material_transport_rates[0, material], sideways_coupling_rate
        )
        stacking_coupling_rate = jnp.where(
            is_material, material_transport_rates[1, material], stacking_coupling_rate
        )
    return jnp.stack([sideways_coupling_rate, stacking_coupling_rate])


def tile_partials(active, tile_hot):
    mesh_height_cells, groups, col_count = active.shape
    quarter = col_count // TILE_COLS
    tile_sums = active.reshape(mesh_height_cells, groups, quarter, TILE_COLS).sum(axis=(0, 3))
    partial_value = exact_dot(tile_sums, tile_hot)
    counts = float(mesh_height_cells * TILE_COLS) * jnp.sum(tile_hot, axis=0)
    return (partial_value, counts)


def spread_power(block_power, tile_hot, mesh_height_cells):
    tile_power = exact_dot(block_power, tile_hot.T)
    groups, quarter = tile_power.shape
    cells = jnp.broadcast_to(
        tile_power[None, :, :, None], (mesh_height_cells, groups, quarter, TILE_COLS)
    )
    return cells.reshape(mesh_height_cells, groups, quarter * TILE_COLS)


def leak_tiers(active, tile_hot, static_power_per_area, warming_power_factor, tier_id):
    partial_value, counts = tile_partials(active, tile_hot)
    block_sum, block_count = lax.psum((partial_value[0], counts), "tile")
    base_row = lax.dynamic_slice_in_dim(static_power_per_area, tier_id, 1, 0)
    slope_row = lax.dynamic_slice_in_dim(warming_power_factor, tier_id, 1, 0)
    return base_row * jnp.exp(slope_row * block_sum[None, :] / block_count[None, :])


def shards(
    starting_warmth_rise,
    substance_per_cell,
    material_transport_rates,
    patch_region_label,
    static_power_per_area,
    warming_power_factor,
    stacking_solve_operator,
):
    mesh_height_cells, stacked_layer_number, lateral_width_cells = starting_warmth_rise.shape
    tier_id = lax.axis_index("tier")
    block_total = static_power_per_area.shape[1]
    codes = substance_per_cell + 1
    block_range = jnp.arange(block_total, dtype=jnp.int32)
    cond_pad = extended(lookup_codes(codes, material_transport_rates), (("tile", 1),), 1)
    cond_pad = jnp.pad(cond_pad, ((0, 0), (0, 0), (0, 0), (1, 1)))
    tile_hot = (patch_region_label[0][:, None] == block_range[None, :]).astype(jnp.float32)
    present_warming_state = starting_warmth_rise
    power_row = jnp.zeros((1, block_total), jnp.float32)
    for step_index in range(STEPS):
        padded = extended(present_warming_state, (("tile", 0),), 1)
        padded = jnp.pad(padded, ((0, 0), (0, 0), (1, 1)))
        power_row = leak_tiers(
            present_warming_state[:, ::stacked_layer_number, :],
            tile_hot,
            static_power_per_area,
            warming_power_factor,
            tier_id,
        )
        moved_field = lateral(padded, cond_pad)
        moved_field = moved_field.at[:, ::stacked_layer_number, :].add(
            SOURCE_GAIN * spread_power(power_row, tile_hot, mesh_height_cells)
        )
        applied = jnp.einsum(
            "lm,rmc->rlc",
            stacking_solve_operator,
            lax.all_to_all(moved_field, "tier", split_axis=2, concat_axis=1, tiled=True),
            precision=lax.Precision.HIGHEST,
        )
        present_warming_state = lax.all_to_all(
            applied, "tier", split_axis=1, concat_axis=2, tiled=True
        )
    return (present_warming_state, power_row)


def solution(mesh):
    in_specs = (
        P("tile", "tier", None),
        P("tile", "tier", None),
        P(),
        P("tile", None),
        P(),
        P(),
        P(),
    )
    out_specs = (P("tile", "tier", None), P("tier", None))
    return jax.shard_map(shards, mesh=mesh, in_specs=in_specs, out_specs=out_specs, check_vma=False)
```

profile of v0, /device:TPU:8, one launch (start us, length us, event | category | flops | bytes accessed | tf_op | source)
XLA Modules:
  0.0 144.2 jit_solution(3918848064363869905)
XLA Ops:
  0.6 0.0 copy-start
  0.6 1.0 fusion.41
  1.6 3.4 %collective-permute-start.3 = (f32[1,24,1024]{2,1,0:T(8,128)S(1)}, f32[1,24,1024]{2,1,0:T(8,128)S(1)}, u32[]{:S(2)}, u32[]{:S(2)}) collective-permute-start(f32[1,24,1024]{2,1,0:T(8,128)S(1)} %get-tuple-element.44), channel_id=1, source_target_pairs={{0,1},{1,2},{2,3},{3,4},{4,5},{5,6},{6,7},{8,9},{9,10},{10,11},{11... | collective-permute-start | bytes 294920 | tf_op jit(solution)/shard_map/ppermute | solution.py:17
  5.0 3.3 %collective-permute-start.1 = (f32[1,24,1024]{2,1,0:T(8,128)S(1)}, f32[1,24,1024]{2,1,0:T(8,128)S(1)}, u32[]{:S(2)}, u32[]{:S(2)}) collective-permute-start(f32[1,24,1024]{2,1,0:T(8,128)S(1)} %get-tuple-element.45), channel_id=1, source_target_pairs={{1,0},{2,1},{3,2},{4,3},{5,4},{6,5},{7,6},{9,8},{10,9},{11,10},{12... | collective-permute-start | bytes 294920 | tf_op jit(solution)/shard_map/ppermute | solution.py:20
  8.4 2.0 %fusion.42 = (f32[1,1]{1,0:T(1,128)}, f32[1,1]{1,0:T(1,128)}, f32[1,1]{1,0:T(1,128)}, f32[1,1]{1,0:T(1,128)}, f32[1,1]{1,0:T(1,128)}, /*index=5*/f32[1,1]{1,0:T(...) fusion(f32[2,8]{1,0:T(2,128)} %param.13), kind=kLoop, calls=%fused_computation.105 | loop fusion | bytes 128 | tf_op jit(solution)/shard_map/slice | solution.py:60
  10.3 6.6 %select_select_fusion = (f32[4,24,1024]{2,1,0:T(8,128)S(1)}, pred[4,24,1024]{2,1,0:T(8,128)(4,1)S(1)}, pred[4,24,1024]{2,1,0:T(8,128)(4,1)S(1)}, pred[4,24,1024]...) fusion(f32[]{:T(128)} %bitcast.16, f32[]{:T(128)} %bitcast.15, ...), kind=kLoop, calls=%fused_computation.62 | loop fusion | flops 1671168 | bytes 1572896 | tf_op jit(solution)/shard_map/jit(_where)/select_n | solution.py:62
  16.9 0.0 copy-start.3
  16.9 0.0 copy-start.7
  16.9 0.0 copy-start.5
  16.9 0.0 copy-start.6
  17.0 5.4 %select_select_fusion.1 = f32[4,24,1024]{2,1,0:T(8,128)S(1)} fusion(pred[4,24,1024]{2,1,0:T(8,128)(4,1)S(1)} %get-tuple-element.39, pred[4,24,1024]{2,1,0:T(8,128)(4,1)S(1)} %get-tuple-element.38, pred[4,24,1024]{2,1,0:T(8,128)(4,1)S(1)} %get-tuple-element.37, pred[4,24,1024]{2,1,0:T(8,128)(4,1)S(1)} %get-tuple-element.36, ...), kind=kLoop, calls=%fused_computation.63 | loop fusion | flops 786432 | bytes 1179680 | tf_op jit(solution)/shard_map/jit(_where)/select_n | solution.py:59
  22.4 2.5 %collective-permute-start.2 = (f32[2,1,24,1024]{3,2,1,0:T(8,128)S(1)}, f32[2,1,24,1024]{3,2,1,0:T(8,128)S(1)}, u32[]{:S(2)}, u32[]{:S(2)}) collective-permute-start(f32[2,1,24,1024]{3,2,1,0:T(8,128)S(1)} %get-tuple-element.40), channel_id=1, source_target_pairs={{0,1},{1,2},{2,3},{3,4},{4,5},{5,6},{6,7},{8,9},{9,10},{10,11},{11... | collective-permute-start | bytes 589832 | tf_op jit(solution)/shard_map/ppermute | solution.py:17
  24.9 4.2 %collective-permute-start = (f32[2,1,24,1024]{3,2,1,0:T(8,128)S(1)}, f32[2,1,24,1024]{3,2,1,0:T(8,128)S(1)}, u32[]{:S(2)}, u32[]{:S(2)}) collective-permute-start(f32[2,1,24,1024]{3,2,1,0:T(8,128)S(1)} %get-tuple-element.41), channel_id=1, source_target_pairs={{1,0},{2,1},{3,2},{4,3},{5,4},{6,5},{7,6},{9,8},{10,9},{11,10},{12... | collective-permute-start | bytes 589832 | tf_op jit(solution)/shard_map/ppermute | solution.py:20
  29.2 0.1 convert_reduce_fusion
  29.3 0.1 bitcast_reduce_fusion.1
  29.4 0.2 fusion.31
  29.6 17.1 %all-reduce.3 = (f32[1,16]{1,0:T(1,128)S(1)}, f32[1,16]{1,0:T(1,128)S(1)}) all-reduce(f32[1,16]{1,0:T(1,128)S(1)} %multiply_bitcast_fusion.2, f32[1,16]{1,0:T(1,128)S(1)} %fusion.31), channel_id=1, replica_groups=mesh['tier'=4,'tile'=8] {'tile'}, use_global_device_ids=true, to_apply=%region_4.5 | all-reduce | flops 32 | bytes 256 | tf_op jit(solution)/shard_map/psum | solution.py:88
  46.7 0.2 fusion.1
  46.8 0.1 broadcast_bitcast_fusion.1
  46.9 0.0 collective-permute-done.3
  46.9 0.0 collective-permute-done.1
  46.9 0.3 select_maximum_fusion.5
  47.2 0.0 collective-permute-done.2
  47.2 0.4 select_maximum_fusion
  47.6 1.2 fusion.18
  48.9 0.1 scatter-add.6
  49.0 0.9 copy.88
  49.9 2.9 %reshape.124 = f32[4,1,24576]{2,1,0:T(1,128)S(1)} reshape(f32[1024,4,24]{2,1,0:T(4,128)S(1)} %bitcast.115) | data formatting | bytes 786432
  52.8 10.0 %all_to_all.72 = f32[4,1,24576]{2,1,0:T(1,128)S(1)} all-to-all(f32[4,1,24576]{2,1,0:T(1,128)S(1)} %reshape.124), channel_id=1, replica_groups=mesh['tier'=4,'tile'=8] {'tier'}, dimensions={0} | all-to-all | bytes 786432 | tf_op jit(solution)/shard_map/all_to_all | solution.py:130
  62.8 0.5 broadcast.157
  63.3 1.7 %reduce.10 = f32[4,24576]{1,0:T(4,128)S(1)} reduce(f32[4,1,24576]{2,1,0:T(1,128)S(1)} %all_to_all.72, f32[]{:T(128)} %broadcast.157), dimensions={1}, to_apply=%all_to_all.52.reduce_sub_computation | reduce | bytes 786436 | tf_op jit(solution)/shard_map/all_to_all | solution.py:130
  65.0 2.8 %reshape.125 = f32[1024,4,24]{2,1,0:T(4,128)S(1)} reshape(f32[4,24576]{1,0:T(4,128)S(1)} %reduce.10) | data formatting | bytes 786432
  67.8 0.8 copy.89
  68.6 0.5 convolution_bitcast_fusion.1
  69.1 0.3 copy.90
  69.4 9.8 %all_to_all.73 = f32[4,96,256]{2,0,1:T(4,128)S(1)} all-to-all(f32[4,96,256]{2,0,1:T(4,128)S(1)} %copy.90), channel_id=1, replica_groups=mesh['tier'=4,'tile'=8] {'tier'}, dimensions={1} | all-to-all | bytes 786432 | tf_op jit(solution)/shard_map/all_to_all | solution.py:133
  79.2 0.3 copy.97
  79.5 0.2 all_to_all.59
  79.7 0.1 bitcast_reduce_fusion
  79.8 0.2 fusion.30
  80.0 0.1 slice.222
  80.1 17.1 %psum.26 = f32[1,16]{1,0:T(1,128)S(1)} all-reduce(f32[1,16]{1,0:T(1,128)S(1)} %fusion.30), channel_id=1, replica_groups=mesh['tier'=4,'tile'=8] {'tile'}, use_global_device_ids=true, to_apply=%region_7.8 | all-reduce | flops 16 | bytes 128 | tf_op jit(solution)/shard_map/psum | solution.py:88
  97.2 0.0 copy-start.4
  97.2 0.2 fusion.2
  97.4 0.1 slice.219
  97.5 6.6 %collective-permute-start.4 = (f32[1,24,1024]{2,1,0:T(8,128)S(1)}, f32[1,24,1024]{2,1,0:T(8,128)S(1)}, u32[]{:S(2)}, u32[]{:S(2)}) collective-permute-start(f32[1,24,1024]{2,1,0:T(8,128)S(1)} %slice.219), channel_id=1, source_target_pairs={{1,0},{2,1},{3,2},{4,3},{5,4},{6,5},{7,6},{9,8},{10,9},{11,10},{12... | collective-permute-start | bytes 294920 | tf_op jit(solution)/shard_map/ppermute | solution.py:20
  104.1 1.9 %collective-permute-start.5 = (f32[1,24,1024]{2,1,0:T(8,128)S(1)}, f32[1,24,1024]{2,1,0:T(8,128)S(1)}, u32[]{:S(2)}, u32[]{:S(2)}) collective-permute-start(f32[1,24,1024]{2,1,0:T(8,128)S(1)} %slice.222), channel_id=1, source_target_pairs={{0,1},{1,2},{2,3},{3,4},{4,5},{5,6},{6,7},{8,9},{9,10},{10,11},{11... | collective-permute-start | bytes 294920 | tf_op jit(solution)/shard_map/ppermute | solution.py:17
  106.0 0.1 broadcast_bitcast_fusion
  106.1 0.2 collective-permute-done.4
  106.3 5.2 %collective-permute-done.5 = f32[1,24,1024]{2,1,0:T(8,128)S(1)} collective-permute-done((f32[1,24,1024]{2,1,0:T(8,128)S(1)}, f32[1,24,1024]{2,1,0:T(8,128)S(1)}, u32[]{:S(2)}, u32[]{:S(2)}) %collective-permute-start.5) | collective-permute-done | bytes 98336 | tf_op jit(solution)/shard_map/ppermute | solution.py:17
  111.5 0.2 select_maximum_fusion.3
  111.8 1.4 fusion.7
  113.2 0.3 scatter-add.9
  113.5 0.9 copy.92
  114.4 2.9 %reshape.126 = f32[4,1,24576]{2,1,0:T(1,128)S(1)} reshape(f32[1024,4,24]{2,1,0:T(4,128)S(1)} %bitcast.117) | data formatting | bytes 786432
  117.3 9.8 %all_to_all.74 = f32[4,1,24576]{2,1,0:T(1,128)S(1)} all-to-all(f32[4,1,24576]{2,1,0:T(1,128)S(1)} %reshape.126), channel_id=1, replica_groups=mesh['tier'=4,'tile'=8] {'tier'}, dimensions={0} | all-to-all | bytes 786432 | tf_op jit(solution)/shard_map/all_to_all | solution.py:130
  127.1 1.7 %reduce.11 = f32[4,24576]{1,0:T(4,128)S(1)} reduce(f32[4,1,24576]{2,1,0:T(1,128)S(1)} %all_to_all.74, f32[]{:T(128)} %broadcast.157), dimensions={1}, to_apply=%all_to_all.60.reduce_sub_computation | reduce | bytes 786436 | tf_op jit(solution)/shard_map/all_to_all | solution.py:130
  128.8 2.8 %reshape.127 = f32[1024,4,24]{2,1,0:T(4,128)S(1)} reshape(f32[4,24576]{1,0:T(4,128)S(1)} %reduce.11) | data formatting | bytes 786432
  131.6 0.8 copy.93
  132.4 0.5 convolution_bitcast_fusion
  132.9 0.3 copy.94
  133.2 9.8 %all_to_all.75 = f32[4,96,256]{2,0,1:T(4,128)S(1)} all-to-all(f32[4,96,256]{2,0,1:T(4,128)S(1)} %copy.94), channel_id=1, replica_groups=mesh['tier'=4,'tile'=8] {'tier'}, dimensions={1} | all-to-all | bytes 786432 | tf_op jit(solution)/shard_map/all_to_all | solution.py:133
  143.0 0.3 copy.95
  143.3 0.9 all_to_all.67
  (19 shorter events, 0.1 us)
Async XLA Ops:
  0.6 68.0 %copy-start = (f32[96,96]{1,0:T(8,128)S(1)}, f32[96,96]{1,0:T(8,128)}, u32[]{:S(2)}) copy-start(f32[96,96]{1,0:T(8,128)} %param.17) | copy-start | bytes 110596
  1.6 45.3 %collective-permute-start.3 = (f32[1,24,1024]{2,1,0:T(8,128)S(1)}, f32[1,24,1024]{2,1,0:T(8,128)S(1)}, u32[]{:S(2)}, u32[]{:S(2)}) collective-permute-start(f32[1,24,1024]{2,1,0:T(8,128)S(1)} %get-tuple-element.44), channel_id=1, source_target_pairs={{0,1},{1,2},{2,3},{3,4},{4,5},{5,6},{6,7},{8,9},{9,10},{10,11},{11... | collective-permute-start | bytes 294920 | tf_op jit(solution)/shard_map/ppermute | solution.py:17
  5.0 41.9 %collective-permute-start.1 = (f32[1,24,1024]{2,1,0:T(8,128)S(1)}, f32[1,24,1024]{2,1,0:T(8,128)S(1)}, u32[]{:S(2)}, u32[]{:S(2)}) collective-permute-start(f32[1,24,1024]{2,1,0:T(8,128)S(1)} %get-tuple-element.45), channel_id=1, source_target_pairs={{1,0},{2,1},{3,2},{4,3},{5,4},{6,5},{7,6},{9,8},{10,9},{11,10},{12... | collective-permute-start | bytes 294920 | tf_op jit(solution)/shard_map/ppermute | solution.py:20
  16.9 12.2 %copy-start.3 = (f32[4,24,1024]{2,1,0:T(8,128)S(1)}, f32[4,24,1024]{2,1,0:T(8,128)}, u32[]{:S(2)}) copy-start(f32[4,24,1024]{2,1,0:T(8,128)} %param.11) | copy-start | bytes 1179652
  16.9 12.2 %copy-start.7 = (s32[1,8]{1,0:T(1,128)S(1)}, s32[1,8]{1,0:T(1,128)}, u32[]{:S(2)}) copy-start(s32[1,8]{1,0:T(1,128)} %param.14) | copy-start | bytes 100
  16.9 29.7 %copy-start.5 = (f32[4,16]{1,0:T(4,128)S(1)}, f32[4,16]{1,0:T(4,128)}, u32[]{:S(2)}) copy-start(f32[4,16]{1,0:T(4,128)} %param.15) | copy-start | bytes 772
  16.9 29.7 %copy-start.6 = (f32[4,16]{1,0:T(4,128)S(1)}, f32[4,16]{1,0:T(4,128)}, u32[]{:S(2)}) copy-start(f32[4,16]{1,0:T(4,128)} %param.16) | copy-start | bytes 772
  22.4 24.8 %collective-permute-start.2 = (f32[2,1,24,1024]{3,2,1,0:T(8,128)S(1)}, f32[2,1,24,1024]{3,2,1,0:T(8,128)S(1)}, u32[]{:S(2)}, u32[]{:S(2)}) collective-permute-start(f32[2,1,24,1024]{3,2,1,0:T(8,128)S(1)} %get-tuple-element.40), channel_id=1, source_target_pairs={{0,1},{1,2},{2,3},{3,4},{4,5},{5,6},{6,7},{8,9},{9,10},{10,11},{11... | collective-permute-start | bytes 589832 | tf_op jit(solution)/shard_map/ppermute | solution.py:17
  24.9 22.3 %collective-permute-start = (f32[2,1,24,1024]{3,2,1,0:T(8,128)S(1)}, f32[2,1,24,1024]{3,2,1,0:T(8,128)S(1)}, u32[]{:S(2)}, u32[]{:S(2)}) collective-permute-start(f32[2,1,24,1024]{3,2,1,0:T(8,128)S(1)} %get-tuple-element.41), channel_id=1, source_target_pairs={{1,0},{2,1},{3,2},{4,3},{5,4},{6,5},{7,6},{9,8},{10,9},{11,10},{12... | collective-permute-start | bytes 589832 | tf_op jit(solution)/shard_map/ppermute | solution.py:20
  47.6 1.3 copy-start.1
  79.5 32.3 %copy-start.2 = (f32[2,6,24,1026]{3,2,1,0:T(8,128)S(1)}, f32[2,6,24,1026]{3,2,1,0:T(8,128)}, u32[]{:S(2)}) copy-start(f32[2,6,24,1026]{3,2,1,0:T(8,128)} %copy-done.1) | copy-start | bytes 3545860
  97.2 16.0 %copy-start.4 = (f32[1,16]{1,0:T(1,128)}, f32[1,16]{1,0:T(1,128)S(1)}, u32[]{:S(2)}) copy-start(f32[1,16]{1,0:T(1,128)S(1)} %exponential_multiply_fusion) | copy-start | bytes 196
  97.5 8.8 %collective-permute-start.4 = (f32[1,24,1024]{2,1,0:T(8,128)S(1)}, f32[1,24,1024]{2,1,0:T(8,128)S(1)}, u32[]{:S(2)}, u32[]{:S(2)}) collective-permute-start(f32[1,24,1024]{2,1,0:T(8,128)S(1)} %slice.219), channel_id=1, source_target_pairs={{1,0},{2,1},{3,2},{4,3},{5,4},{6,5},{7,6},{9,8},{10,9},{11,10},{12... | collective-permute-start | bytes 294920 | tf_op jit(solution)/shard_map/ppermute | solution.py:20
  104.1 7.4 %collective-permute-start.5 = (f32[1,24,1024]{2,1,0:T(8,128)S(1)}, f32[1,24,1024]{2,1,0:T(8,128)S(1)}, u32[]{:S(2)}, u32[]{:S(2)}) collective-permute-start(f32[1,24,1024]{2,1,0:T(8,128)S(1)} %slice.222), channel_id=1, source_target_pairs={{0,1},{1,2},{2,3},{3,4},{4,5},{5,6},{6,7},{8,9},{9,10},{10,11},{11... | collective-permute-start | bytes 294920 | tf_op jit(solution)/shard_map/ppermute | solution.py:17
where the time goes:
time: 145 us; the launch traced here: 144 us
  blocking collectives  73.7 us (51%)
  starting transfers between devices  22 us (15%)
  local copies, waits for them, and re-layouts  21 us (14%)
  other arithmetic  19.3 us (13%)
  waiting for transfers between devices  5.42 us (4%)
  matrix products  1.71 us (1%)
    psum x2, blocking collectives, leak_tiers(): block_sum, block_count = lax.psum((partial_value[0], counts), 'tile')  34.2 us
    all_to_all x2, blocking collectives, shards(): lax.all_to_all(moved_field, 'tier', split_axis=2, concat_axis=1, tiled=True)  19.8 us
    all_to_all x2, blocking collectives, shards(): lax.all_to_all(applied, 'tier', split_axis=1, concat_axis=2, tiled=True)  19.7 us
    ppermute x3, starting transfers between devices, extended(): lax.ppermute(lax.slice_in_dim(block, 0, width, axis=dim), axis, backward)  14.1 us
    unnamed x20, local copies, waits for them, and re-layouts  11.4 us
    ppermute x3, starting transfers between devices, extended(): lax.ppermute(lax.slice_in_dim(block, block.shape[dim] - width, None, axis...  7.88 us
    select_n x1, other arithmetic, lookup_codes(): jnp.where(is_material, material_transport_rates[1, material], stacking_co...  6.55 us
    select_n x1, other arithmetic, lookup_codes(): jnp.where(is_material, material_transport_rates[0, material], sideways_co...  5.36 us
  transfers between devices with their start and end apart: 6, of which 2 were waited for; matrix products, arithmetic and copies ran while one was open for 10% of the time, Pallas kernels for 0%

commit v1 on v0

--- a/solution.py
+++ b/solution.py
@@ -130,8 +130,11 @@
             lax.all_to_all(moved_field, "tier", split_axis=2, concat_axis=1, tiled=True),
             precision=lax.Precision.HIGHEST,
         )
-        present_warming_state = lax.all_to_all(
-            applied, "tier", split_axis=1, concat_axis=2, tiled=True
+        present_warming_state = jnp.concatenate(
+            lax.all_to_all(
+                jnp.stack(jnp.split(applied, lax.axis_size("tier"), axis=1)), "tier", 0, 0
+            ),
+            axis=2,
         )
     return (present_warming_state, power_row)
 

time: 145 us -> 140 us (0.966)
  the two profiles are of different devices: /device:TPU:8 before, /device:TPU:0 now
where the time goes in v1:
time: 140 us
  blocking collectives  79.9 us (57%)
  local copies, waits for them, and re-layouts  19.6 us (14%)
  other arithmetic  19.4 us (14%)
  starting transfers between devices  18 us (13%)
  matrix products  1.71 us (1%)
    psum x2, blocking collectives, leak_tiers(): block_sum, block_count = lax.psum((partial_value[0], counts), 'tile')  40.4 us
    all_to_all x2, blocking collectives, shards(): lax.all_to_all(moved_field, 'tier', split_axis=2, concat_axis=1, tiled=True)  19.8 us
    all_to_all x2, blocking collectives, shards(): lax.all_to_all(jnp.stack(jnp.split(applied, lax.axis_size('tier'), axis=1...  19.7 us
    ppermute x3, starting transfers between devices, extended(): lax.ppermute(lax.slice_in_dim(block, block.shape[dim] - width, None, axis...  14 us
    unnamed x21, local copies, waits for them, and re-layouts  11.4 us
    select_n x1, other arithmetic, lookup_codes(): jnp.where(is_material, material_transport_rates[1, material], stacking_co...  6.55 us
    select_n x1, other arithmetic, lookup_codes(): jnp.where(is_material, material_transport_rates[0, material], sideways_co...  5.36 us
    ppermute x3, starting transfers between devices, extended(): lax.ppermute(lax.slice_in_dim(block, 0, width, axis=dim), axis, backward)  4.01 us
  transfers between devices with their start and end apart: 6, of which 0 were waited for; matrix products, arithmetic and copies ran while one was open for 11% of the time, Pallas kernels for 0%

profile of v1, /device:TPU:0, one launch (start us, length us, event | category | flops | bytes accessed | tf_op | source)
XLA Modules:
  0.0 139.7 jit_solution(6274307665839104735)
XLA Ops:
  0.6 0.0 copy-start
  0.6 1.0 fusion.40
  1.6 4.9 %collective-permute-start.3 = (f32[1,24,1024]{2,1,0:T(8,128)S(1)}, f32[1,24,1024]{2,1,0:T(8,128)S(1)}, u32[]{:S(2)}, u32[]{:S(2)}) collective-permute-start(f32[1,24,1024]{2,1,0:T(8,128)S(1)} %get-tuple-element.52), channel_id=1, source_target_pairs={{0,1},{1,2},{2,3},{3,4},{4,5},{5,6},{6,7},{8,9},{9,10},{10,11},{11... | collective-permute-start | bytes 294920 | tf_op jit(solution)/shard_map/ppermute | solution.py:17
  6.5 1.3 collective-permute-start.1
  7.8 2.0 %fusion.41 = (f32[1,1]{1,0:T(1,128)}, f32[1,1]{1,0:T(1,128)}, f32[1,1]{1,0:T(1,128)}, f32[1,1]{1,0:T(1,128)}, f32[1,1]{1,0:T(1,128)}, /*index=5*/f32[1,1]{1,0:T(...) fusion(f32[2,8]{1,0:T(2,128)} %param.13), kind=kLoop, calls=%fused_computation.115 | loop fusion | bytes 128 | tf_op jit(solution)/shard_map/slice | solution.py:60
  9.8 6.6 %select_select_fusion = (f32[4,24,1024]{2,1,0:T(8,128)S(1)}, pred[4,24,1024]{2,1,0:T(8,128)(4,1)S(1)}, pred[4,24,1024]{2,1,0:T(8,128)(4,1)S(1)}, pred[4,24,1024]...) fusion(f32[]{:T(128)} %bitcast.16, f32[]{:T(128)} %bitcast.15, ...), kind=kLoop, calls=%fused_computation.63 | loop fusion | flops 1671168 | bytes 1572896 | tf_op jit(solution)/shard_map/jit(_where)/select_n | solution.py:62
  16.3 0.0 copy-start.3
  16.3 0.0 copy-start.7
  16.4 0.0 copy-start.5
  16.4 0.0 copy-start.6
  16.4 5.4 %select_select_fusion.1 = f32[4,24,1024]{2,1,0:T(8,128)S(1)} fusion(pred[4,24,1024]{2,1,0:T(8,128)(4,1)S(1)} %get-tuple-element.39, pred[4,24,1024]{2,1,0:T(8,128)(4,1)S(1)} %get-tuple-element.38, pred[4,24,1024]{2,1,0:T(8,128)(4,1)S(1)} %get-tuple-element.37, pred[4,24,1024]{2,1,0:T(8,128)(4,1)S(1)} %get-tuple-element.36, ...), kind=kLoop, calls=%fused_computation.64 | loop fusion | flops 786432 | bytes 1179680 | tf_op jit(solution)/shard_map/jit(_where)/select_n | solution.py:59
  21.8 4.6 %collective-permute-start.2 = (f32[2,1,24,1024]{3,2,1,0:T(8,128)S(1)}, f32[2,1,24,1024]{3,2,1,0:T(8,128)S(1)}, u32[]{:S(2)}, u32[]{:S(2)}) collective-permute-start(f32[2,1,24,1024]{3,2,1,0:T(8,128)S(1)} %get-tuple-element.40), channel_id=1, source_target_pairs={{0,1},{1,2},{2,3},{3,4},{4,5},{5,6},{6,7},{8,9},{9,10},{10,11},{11... | collective-permute-start | bytes 589832 | tf_op jit(solution)/shard_map/ppermute | solution.py:17
  26.3 1.3 collective-permute-start
  27.7 0.0 copy-done.3
  27.7 0.0 copy-done.7
  27.7 0.1 convert_reduce_fusion
  27.8 0.1 bitcast_reduce_fusion.1
  27.9 0.2 fusion.31
  28.1 22.8 %all-reduce.3 = (f32[1,16]{1,0:T(1,128)S(1)}, f32[1,16]{1,0:T(1,128)S(1)}) all-reduce(f32[1,16]{1,0:T(1,128)S(1)} %multiply_bitcast_fusion.2, f32[1,16]{1,0:T(1,128)S(1)} %fusion.31), channel_id=1, replica_groups=mesh['tier'=4,'tile'=8] {'tile'}, use_global_device_ids=true, to_apply=%region_4.5 | all-reduce | flops 32 | bytes 256 | tf_op jit(solution)/shard_map/psum | solution.py:88
  50.9 0.0 copy-done.5
  50.9 0.0 copy-done.6
  50.9 0.2 fusion.1
  51.1 0.1 broadcast_bitcast_fusion.1
  51.1 0.0 collective-permute-done.3
  51.1 0.0 collective-permute-done.1
  51.2 0.3 select_maximum_fusion.5
  51.4 0.0 collective-permute-done.2
  51.4 0.0 collective-permute-done
  51.4 0.4 select_maximum_fusion
  51.8 0.0 copy-start.1
  51.9 1.2 fusion.18
  53.1 0.0 copy-done.1
  53.1 0.1 scatter-add.6
  53.3 0.9 copy.25
  54.1 2.9 %reshape.140 = f32[4,1,24576]{2,1,0:T(1,128)S(1)} reshape(f32[1024,4,24]{2,1,0:T(4,128)S(1)} %bitcast.136) | data formatting | bytes 786432
  57.0 10.0 %all_to_all.46 = f32[4,1,24576]{2,1,0:T(1,128)S(1)} all-to-all(f32[4,1,24576]{2,1,0:T(1,128)S(1)} %reshape.140), channel_id=1, replica_groups=mesh['tier'=4,'tile'=8] {'tier'}, dimensions={0} | all-to-all | bytes 786432 | tf_op jit(solution)/shard_map/all_to_all | solution.py:130
  67.0 0.5 broadcast.157
  67.5 1.7 %reduce.10 = f32[4,24576]{1,0:T(4,128)S(1)} reduce(f32[4,1,24576]{2,1,0:T(1,128)S(1)} %all_to_all.46, f32[]{:T(128)} %broadcast.157), dimensions={1}, to_apply=%all_to_all.32.reduce_sub_computation | reduce | bytes 786436 | tf_op jit(solution)/shard_map/all_to_all | solution.py:130
  69.3 2.8 %reshape.141 = f32[1024,4,24]{2,1,0:T(4,128)S(1)} reshape(f32[4,24576]{1,0:T(4,128)S(1)} %reduce.10) | data formatting | bytes 786432
  72.1 0.8 copy.26
  72.8 0.5 convolution_bitcast_fusion.1
  73.4 9.8 %all_to_all.47 = f32[4,4,24,256]{3,2,1,0:T(8,128)S(1)} all-to-all(f32[4,4,24,256]{3,2,1,0:T(8,128)S(1)} %pad_maximum_fusion.8), channel_id=1, replica_groups=mesh['tier'=4,'tile'=8] {'tier'}, dimensions={0} | all-to-all | bytes 786432 | tf_op jit(solution)/shard_map/all_to_all | solution.py:134
  83.3 1.4 %collective-permute-start.4 = (f32[1,24,1024]{2,1,0:T(8,128)S(1)}, f32[1,24,1024]{2,1,0:T(8,128)S(1)}, u32[]{:S(2)}, u32[]{:S(2)}) collective-permute-start(f32[1,24,1024]{2,1,0:T(8,128)S(1)} %bitcast.150), channel_id=1, source_target_pairs={{1,0},{2,1},{3,2},{4,3},{5,4},{6,5},{7,6},{9,8},{10,9},{11,10},{12... | collective-permute-start | bytes 294920 | tf_op jit(solution)/shard_map/ppermute | solution.py:20
  84.8 0.1 bitcast_reduce_fusion
  84.9 0.2 fusion.30
  85.1 4.5 %collective-permute-start.5 = (f32[1,24,1024]{2,1,0:T(8,128)S(1)}, f32[1,24,1024]{2,1,0:T(8,128)S(1)}, u32[]{:S(2)}, u32[]{:S(2)}) collective-permute-start(f32[1,24,1024]{2,1,0:T(8,128)S(1)} %bitcast.149), channel_id=1, source_target_pairs={{0,1},{1,2},{2,3},{3,4},{4,5},{5,6},{6,7},{8,9},{9,10},{10,11},{11... | collective-permute-start | bytes 294920 | tf_op jit(solution)/shard_map/ppermute | solution.py:17
  89.7 17.6 %psum.26 = f32[1,16]{1,0:T(1,128)S(1)} all-reduce(f32[1,16]{1,0:T(1,128)S(1)} %fusion.30), channel_id=1, replica_groups=mesh['tier'=4,'tile'=8] {'tile'}, use_global_device_ids=true, to_apply=%region_7.8 | all-reduce | flops 16 | bytes 128 | tf_op jit(solution)/shard_map/psum | solution.py:88
  107.3 0.0 copy-start.4
  107.3 0.2 fusion.2
  107.5 0.1 broadcast_bitcast_fusion
  107.6 0.0 collective-permute-done.4
  107.6 0.0 collective-permute-done.5
  107.6 0.2 select_maximum_fusion.3
  107.9 1.4 %fusion.7 = f32[4,24,1024]{2,1,0:T(8,128)S(1)} fusion(f32[4,24,1024]{2,1,0:T(8,128)S(1)} %bitcast.142, f32[6,24,1026]{2,1,0:T(8,128)S(1)} %select_maximum_fusion.3, f32[4,24,1024]{2,1,0:T(8,128)} %get-tuple-element.30, f32[1,24,1024]{2,1,0:T(8,128)S(1)} %collective-permute-done.5, f32[4,24,1024]{2,1,0:T(8,128)S(1)} %get-tuple-element.29, ...), kind=kLoop, calls=%fused_computation.23 | loop fusion | flops 2162688 | bytes 3735552 | tf_op jit(solution)/shard_map/add | solution.py:45
  109.3 0.3 scatter-add.9
  109.6 0.9 copy.30
  110.5 2.9 %reshape.142 = f32[4,1,24576]{2,1,0:T(1,128)S(1)} reshape(f32[1024,4,24]{2,1,0:T(4,128)S(1)} %bitcast.138) | data formatting | bytes 786432
  113.4 9.8 %all_to_all.48 = f32[4,1,24576]{2,1,0:T(1,128)S(1)} all-to-all(f32[4,1,24576]{2,1,0:T(1,128)S(1)} %reshape.142), channel_id=1, replica_groups=mesh['tier'=4,'tile'=8] {'tier'}, dimensions={0} | all-to-all | bytes 786432 | tf_op jit(solution)/shard_map/all_to_all | solution.py:130
  123.2 1.7 %reduce.11 = f32[4,24576]{1,0:T(4,128)S(1)} reduce(f32[4,1,24576]{2,1,0:T(1,128)S(1)} %all_to_all.48, f32[]{:T(128)} %broadcast.157), dimensions={1}, to_apply=%all_to_all.37.reduce_sub_computation | reduce | bytes 786436 | tf_op jit(solution)/shard_map/all_to_all | solution.py:130
  124.9 2.8 %reshape.143 = f32[1024,4,24]{2,1,0:T(4,128)S(1)} reshape(f32[4,24576]{1,0:T(4,128)S(1)} %reduce.11) | data formatting | bytes 786432
  127.7 0.8 copy.31
  128.5 0.5 convolution_bitcast_fusion
  129.1 9.8 %all_to_all.49 = f32[4,4,24,256]{3,2,1,0:T(8,128)S(1)} all-to-all(f32[4,4,24,256]{3,2,1,0:T(8,128)S(1)} %pad_maximum_fusion.9), channel_id=1, replica_groups=mesh['tier'=4,'tile'=8] {'tier'}, dimensions={0} | all-to-all | bytes 786432 | tf_op jit(solution)/shard_map/all_to_all | solution.py:134
  138.9 0.8 copy.36
  (19 shorter events, 0.3 us)
Async XLA Ops:
  0.6 72.2 %copy-start = (f32[96,96]{1,0:T(8,128)S(1)}, f32[96,96]{1,0:T(8,128)}, u32[]{:S(2)}) copy-start(f32[96,96]{1,0:T(8,128)} %param.17) | copy-start | bytes 110596
  1.6 49.5 %collective-permute-start.3 = (f32[1,24,1024]{2,1,0:T(8,128)S(1)}, f32[1,24,1024]{2,1,0:T(8,128)S(1)}, u32[]{:S(2)}, u32[]{:S(2)}) collective-permute-start(f32[1,24,1024]{2,1,0:T(8,128)S(1)} %get-tuple-element.52), channel_id=1, source_target_pairs={{0,1},{1,2},{2,3},{3,4},{4,5},{5,6},{6,7},{8,9},{9,10},{10,11},{11... | collective-permute-start | bytes 294920 | tf_op jit(solution)/shard_map/ppermute | solution.py:17
  6.5 44.7 %collective-permute-start.1 = (f32[1,24,1024]{2,1,0:T(8,128)S(1)}, f32[1,24,1024]{2,1,0:T(8,128)S(1)}, u32[]{:S(2)}, u32[]{:S(2)}) collective-permute-start(f32[1,24,1024]{2,1,0:T(8,128)S(1)} %get-tuple-element.53), channel_id=1, source_target_pairs={{1,0},{2,1},{3,2},{4,3},{5,4},{6,5},{7,6},{9,8},{10,9},{11,10},{12... | collective-permute-start | bytes 294920 | tf_op jit(solution)/shard_map/ppermute | solution.py:20
  16.3 11.3 %copy-start.3 = (f32[4,24,1024]{2,1,0:T(8,128)S(1)}, f32[4,24,1024]{2,1,0:T(8,128)}, u32[]{:S(2)}) copy-start(f32[4,24,1024]{2,1,0:T(8,128)} %param.11) | copy-start | bytes 1179652
  16.3 11.3 %copy-start.7 = (s32[1,8]{1,0:T(1,128)S(1)}, s32[1,8]{1,0:T(1,128)}, u32[]{:S(2)}) copy-start(s32[1,8]{1,0:T(1,128)} %param.14) | copy-start | bytes 100
  16.4 34.5 %copy-start.5 = (f32[4,16]{1,0:T(4,128)S(1)}, f32[4,16]{1,0:T(4,128)}, u32[]{:S(2)}) copy-start(f32[4,16]{1,0:T(4,128)} %param.15) | copy-start | bytes 772
  16.4 34.5 %copy-start.6 = (f32[4,16]{1,0:T(4,128)S(1)}, f32[4,16]{1,0:T(4,128)}, u32[]{:S(2)}) copy-start(f32[4,16]{1,0:T(4,128)} %param.16) | copy-start | bytes 772
  21.8 29.6 %collective-permute-start.2 = (f32[2,1,24,1024]{3,2,1,0:T(8,128)S(1)}, f32[2,1,24,1024]{3,2,1,0:T(8,128)S(1)}, u32[]{:S(2)}, u32[]{:S(2)}) collective-permute-start(f32[2,1,24,1024]{3,2,1,0:T(8,128)S(1)} %get-tuple-element.40), channel_id=1, source_target_pairs={{0,1},{1,2},{2,3},{3,4},{4,5},{5,6},{6,7},{8,9},{9,10},{10,11},{11... | collective-permute-start | bytes 589832 | tf_op jit(solution)/shard_map/ppermute | solution.py:17
  26.3 25.1 %collective-permute-start = (f32[2,1,24,1024]{3,2,1,0:T(8,128)S(1)}, f32[2,1,24,1024]{3,2,1,0:T(8,128)S(1)}, u32[]{:S(2)}, u32[]{:S(2)}) collective-permute-start(f32[2,1,24,1024]{3,2,1,0:T(8,128)S(1)} %get-tuple-element.41), channel_id=1, source_target_pairs={{1,0},{2,1},{3,2},{4,3},{5,4},{6,5},{7,6},{9,8},{10,9},{11,10},{12... | collective-permute-start | bytes 589832 | tf_op jit(solution)/shard_map/ppermute | solution.py:20
  51.8 1.3 copy-start.1
  83.3 24.6 %copy-start.2 = (f32[2,6,24,1026]{3,2,1,0:T(8,128)S(1)}, f32[2,6,24,1026]{3,2,1,0:T(8,128)}, u32[]{:S(2)}) copy-start(f32[2,6,24,1026]{3,2,1,0:T(8,128)} %copy-done.1) | copy-start | bytes 3545860
  83.3 24.3 %collective-permute-start.4 = (f32[1,24,1024]{2,1,0:T(8,128)S(1)}, f32[1,24,1024]{2,1,0:T(8,128)S(1)}, u32[]{:S(2)}, u32[]{:S(2)}) collective-permute-start(f32[1,24,1024]{2,1,0:T(8,128)S(1)} %bitcast.150), channel_id=1, source_target_pairs={{1,0},{2,1},{3,2},{4,3},{5,4},{6,5},{7,6},{9,8},{10,9},{11,10},{12... | collective-permute-start | bytes 294920 | tf_op jit(solution)/shard_map/ppermute | solution.py:20
  85.1 22.5 %collective-permute-start.5 = (f32[1,24,1024]{2,1,0:T(8,128)S(1)}, f32[1,24,1024]{2,1,0:T(8,128)S(1)}, u32[]{:S(2)}, u32[]{:S(2)}) collective-permute-start(f32[1,24,1024]{2,1,0:T(8,128)S(1)} %bitcast.149), channel_id=1, source_target_pairs={{0,1},{1,2},{2,3},{3,4},{4,5},{5,6},{6,7},{8,9},{9,10},{10,11},{11... | collective-permute-start | bytes 294920 | tf_op jit(solution)/shard_map/ppermute | solution.py:17
  107.3 1.9 %copy-start.4 = (f32[1,16]{1,0:T(1,128)}, f32[1,16]{1,0:T(1,128)S(1)}, u32[]{:S(2)}) copy-start(f32[1,16]{1,0:T(1,128)S(1)} %exponential_multiply_fusion) | copy-start | bytes 196
